TPU v7x, 256 devices: a whole 4x4x8 slice. The times are simulated.
256 devices in a mesh: segment: 2 (over y_hi), seq: 128 (over z, x, y_lo, core).
Axes of the slice: x: 4, y: 4 (y_hi: 2, y_lo: 2; y = y_hi * 2 + y_lo), z: 8, core: 2. Of those that a mesh axis runs over, the one named last changes fastest.
Arguments:
- latent: bfloat16 [32768, 5120], P('seq'), may hold values from -6 to 6
- stale_hidden: bfloat16 [32768, 5120], P('seq'), may hold values from -6 to 6
- step_ids: int32 [3], replicated, may hold values from 0 to 999, as said below
- sigma_table: int32 [1000], replicated, may hold values from 1 to 1000, as said below
- mod_weight: bfloat16 [2, 256, 15360], P('segment', None, 'seq'), may hold values from -0.375 to 0.375
Outputs:
- latent_next: bfloat16 [32768, 5120], P('seq')
- hidden_last: bfloat16 [32768, 5120], P('seq')
Inputs may be any that keep to these rules, and one draw needn't show every extreme that they name: `step_ids`: strictly falling along the steps. `sigma_table`: never falling along the table.
All inputs are finite; a program needn't handle non-finite values.
Results may differ from a plain program's by a relative error of at most 0.014.
Values may be sent and summed in bfloat16 or wider, within the bound.
A program may use at most 128 MiB of HBM per device.

v0:
```python
import math

import jax
import jax.numpy as jnp
from jax import lax
from jax.sharding import PartitionSpec as P

HEADS = 40
WINDOW = 128
STEPS = 2


def padded(block, sides, width):
    for axis, dim in sides:
        count = lax.axis_size(axis)
        forward = [(i, i + 1) for i in range(count - 1)]
        backward = [(target, source) for source, target in forward]
        low = lax.ppermute(
            lax.slice_in_dim(block, block.shape[dim] - width, None, axis=dim), axis, forward
        )
        high = lax.ppermute(lax.slice_in_dim(block, 0, width, axis=dim), axis, backward)
        block = jnp.concatenate([low, block, high], axis=dim)
    return block


def from_partner(value, axis, distance):
    mask = 2**distance
    pairs = [(source, source ^ mask) for source in range(lax.axis_size(axis))]
    return lax.ppermute(value, axis, pairs)


def embed(t_value, count):
    half = count // 2
    freqs = jnp.exp(-math.log(10000.0) * jnp.arange(half, dtype=jnp.float32) / half)
    angles = t_value * freqs
    return jnp.concatenate([jnp.cos(angles), jnp.sin(angles)])


def section(hidden, t_value, mod_w, start, total):
    rows, width = hidden.shape
    heads = HEADS
    head = width // heads
    features = jax.nn.silu(embed(t_value, mod_w.shape[0])).astype(jnp.bfloat16)
    columns = jnp.dot(features, mod_w, preferred_element_type=jnp.float32)
    mod = lax.all_gather(columns, "seq", axis=0, tiled=True)
    shift = mod[:width]
    scale = mod[width : 2 * width]
    gate = mod[2 * width :]
    values = hidden.astype(jnp.float32)
    mean = jnp.mean(values, axis=-1, keepdims=True)
    var = jnp.mean((values - mean) ** 2, axis=-1, keepdims=True)
    normed = ((values - mean) * lax.rsqrt(var + 1e-06) * (1.0 + scale) + shift).astype(jnp.bfloat16)
    by_head = normed.reshape(rows, heads, head)
    widened = padded(by_head, (("seq", 0),), rows)
    keys = widened[rows - WINDOW : 2 * rows + WINDOW]
    span = rows + 2 * WINDOW
    qpos = start + jnp.arange(rows, dtype=jnp.int32)
    kpos = start - WINDOW + jnp.arange(span, dtype=jnp.int32)
    dist = qpos[:, None] - kpos[None, :]
    allowed = (jnp.abs(dist) <= WINDOW) & (kpos[None, :] >= 0) & (kpos[None, :] < total)
    scores = jnp.einsum("qhd,khd->hqk", by_head, keys, preferred_element_type=jnp.float32) / float(
        head
    )
    scores = jnp.where(allowed[None], scores, -jnp.inf)
    top = jnp.max(scores, axis=-1, keepdims=True)
    expo = jnp.exp(scores - top)
    probs = (expo / jnp.sum(expo, axis=-1, keepdims=True)).astype(jnp.bfloat16)
    attn = jnp.einsum("hqk,khd->qhd", probs, keys, preferred_element_type=jnp.float32)
    attn = attn.astype(jnp.bfloat16).reshape(rows, width)
    return (values + gate * attn.astype(jnp.float32)).astype(jnp.bfloat16)


def per_device(latent, stale_hidden, step_ids, sigma_table, mod_weight):
    rows = latent.shape[0]
    first = lax.axis_index("segment") == 0
    start = lax.axis_index("seq") * rows
    total = rows * lax.axis_size("seq")
    mod_w = mod_weight[0]
    state = latent
    hidden = stale_hidden
    for step in range(STEPS):
        t_now = sigma_table[step_ids[step]].astype(jnp.float32)
        t_next = sigma_table[step_ids[step + 1]].astype(jnp.float32)
        source = jnp.where(first, state, hidden)
        result = section(source, t_now, mod_w, start, total)
        partner = from_partner(result, "segment", 0)
        fresh = jnp.where(first, result, partner)
        noise = jnp.where(first, partner, result)
        state = (
            state.astype(jnp.float32) + (t_next - t_now) / 1000.0 * noise.astype(jnp.float32)
        ).astype(jnp.bfloat16)
        hidden = fresh
    return (state, hidden)


def solution(mesh):
    placed = (P("seq", None), P("seq", None), P(), P(), P("segment", None, "seq"))
    return jax.shard_map(
        per_device,
        mesh=mesh,
        in_specs=placed,
        out_specs=(P("seq", None), P("seq", None)),
        check_vma=False,
    )
```

profile of v0, /device:TPU:1, one launch (start us, length us, event | category | flops | bytes accessed | tf_op | source)
XLA Modules:
  0.0 1277.8 jit_solution(4613282809551016996)
XLA Ops:
  7.2 1.4 fusion.51
  14.4 1.4 fusion.50
  20.8 3.0 copy.11
  23.7 4.4 copy.13
  29.2 1.5 copy-done.2
  31.4 930.2 %all-reduce.5.cloned.1.call-done = (f32[15360]{0:T(1024)}, f32[15360]{0:T(1024)}) async-done(((f32[15360]{0:T(1024)}, f32[15360]{0:T(1024)}), (f32[15360]{0:T(1024)}, f32[15360]{0:T(1024)})) %all-reduce.5.cloned.1.call-update) | async-done | bytes 122896
  962.3 5.4 fusion.23
  967.7 4.4 copy.14
  972.1 5.2 collective-permute-start.1
  977.3 1.9 collective-permute-start
  979.5 25.9 %collective-permute-done.1 = bf16[256,40,128]{2,0,1:T(8,128)(2,1)} collective-permute-done((bf16[256,40,128]{2,0,1:T(8,128)(2,1)}, bf16[256,40,128]{2,0,1:T(8,128)(2,1)}, u32[]{:S(2)}, u32[]{:S(2)}) %collective-permute-start.1) | collective-permute-done | bytes 2621472 | tf_op jit(solution)/shard_map/ppermute | solution.py:21
  1005.3 37.9 %collective-permute-done = bf16[256,40,128]{2,0,1:T(8,128)(2,1)} collective-permute-done((bf16[256,40,128]{2,0,1:T(8,128)(2,1)}, bf16[256,40,128]{2,0,1:T(8,128)(2,1)}, u32[]{:S(2)}, u32[]{:S(2)}) %collective-permute-start) | collective-permute-done | bytes 2621472 | tf_op jit(solution)/shard_map/ppermute | solution.py:18
  1043.3 13.4 %fusion.52 = (f32[40,256]{1,0:T(8,128)S(1)}, f32[40,256,512]{2,1,0:T(8,128)}) fusion(pred[256,512]{1,0:T(8,128)(4,1)S(1)} %fusion.31, bf16[256,40,128]{0,2,1:T(8,128)(2,1)} %bitcast.37, bf16[256,40,128]{2,0,1:T(8,128)(2,1)} %collective-permute-done.1, bf16[256,40,128]{2,0,1:T(8,128)(2,1)} %copy.14, bf16[256,40,128]{2,0,1:T(8,128)(2,1)} %collective-permute-done), kind=kOutput, calls=%fused_computation.91 | convolution fusion | flops 1378877952 | bytes 31629312 | tf_op jit(solution)/shard_map/sub | solution.py:66
  1056.7 13.0 %convert_convert_fusion.1 = f32[40,128,256]{2,1,0:T(8,128)} fusion(f32[40,256,512]{2,1,0:T(8,128)} %get-tuple-element.23, f32[40,256]{1,0:T(8,128)S(1)} %get-tuple-element.22, bf16[256,40,128]{2,0,1:T(8,128)(2,1)} %collective-permute-done.1, bf16[256,40,128]{2,0,1:T(8,128)(2,1)} %copy.14, bf16[256,40,128]{2,0,1:T(8,128)(2,1)} %collective-permute-done), kind=kOutput, calls=%fused_computation.48 | convolution fusion | flops 1371013120 | bytes 34119680 | tf_op jit(solution)/shard_map/hqk,khd->qhd/dot_general | solution.py:68
  1069.7 5.5 fusion.24
  1075.2 4.3 collective-permute-start.2
  1079.5 57.4 %collective-permute-done.2 = bf16[256,5120]{0,1:T(8,128)(2,1)} collective-permute-done((bf16[256,5120]{0,1:T(8,128)(2,1)}, bf16[256,5120]{0,1:T(8,128)(2,1)}, u32[]{:S(2)}, u32[]{:S(2)}) %collective-permute-start.2) | collective-permute-done | bytes 2621472 | tf_op jit(solution)/shard_map/ppermute | solution.py:29
  1137.0 4.2 convert_reduce_fusion
  1142.6 3.7 fusion.19
  1146.3 4.4 copy.19
  1150.7 1.9 collective-permute-start.4
  1152.6 3.6 collective-permute-start.3
  1156.3 27.7 %collective-permute-done.4 = bf16[256,40,128]{2,0,1:T(8,128)(2,1)} collective-permute-done((bf16[256,40,128]{2,0,1:T(8,128)(2,1)}, bf16[256,40,128]{2,0,1:T(8,128)(2,1)}, u32[]{:S(2)}, u32[]{:S(2)}) %collective-permute-start.4) | collective-permute-done | bytes 2621472 | tf_op jit(solution)/shard_map/ppermute | solution.py:21
  1185.2 13.4 %fusion.53 = (f32[40,256]{1,0:T(8,128)S(1)}, f32[40,256,512]{2,1,0:T(8,128)}) fusion(pred[256,512]{1,0:T(8,128)(4,1)S(1)} %fusion.31, bf16[256,40,128]{0,2,1:T(8,128)(2,1)} %bitcast.39, bf16[256,40,128]{2,0,1:T(8,128)(2,1)} %collective-permute-done.4, bf16[256,40,128]{2,0,1:T(8,128)(2,1)} %copy.19, bf16[256,40,128]{2,0,1:T(8,128)(2,1)} %collective-permute-done.3), kind=kOutput, calls=%fused_computation.92 | convolution fusion | flops 1378877952 | bytes 31629312 | tf_op jit(solution)/shard_map/sub | solution.py:66
  1198.6 13.0 %convert_convert_fusion = f32[40,128,256]{2,1,0:T(8,128)} fusion(f32[40,256,512]{2,1,0:T(8,128)} %get-tuple-element.25, f32[40,256]{1,0:T(8,128)S(1)} %get-tuple-element.24, bf16[256,40,128]{2,0,1:T(8,128)(2,1)} %collective-permute-done.4, bf16[256,40,128]{2,0,1:T(8,128)(2,1)} %copy.19, bf16[256,40,128]{2,0,1:T(8,128)(2,1)} %collective-permute-done.3), kind=kOutput, calls=%fused_computation.46 | convolution fusion | flops 1371013120 | bytes 34119680 | tf_op jit(solution)/shard_map/hqk,khd->qhd/dot_general | solution.py:68
  1211.6 5.5 fusion.25
  1217.1 3.0 collective-permute-start.5
  1220.7 32.0 %collective-permute-done.5 = bf16[256,5120]{0,1:T(8,128)(2,1)} collective-permute-done((bf16[256,5120]{0,1:T(8,128)(2,1)}, bf16[256,5120]{0,1:T(8,128)(2,1)}, u32[]{:S(2)}, u32[]{:S(2)}) %collective-permute-start.5) | collective-permute-done | bytes 2621472 | tf_op jit(solution)/shard_map/ppermute | solution.py:29
  1252.7 3.5 broadcast_select_fusion
  1256.2 4.4 copy.25
  1260.6 6.0 add_convert_fusion
  1266.6 4.4 copy.24
  (42 shorter events, 8.4 us)
Async XLA Ops:
  7.2 10.2 copy-start
  7.2 954.4 %all-reduce.5.cloned.1.call-start = ((), (), s32[]{:S(2)}) async-start(), calls=%async_computation | async-start | bytes 245760
  19.8 0.6 copy-start.5
  20.1 0.6 copy-start.4
  29.1 1.5 copy-start.2
  972.1 33.3 %collective-permute-start.1 = (bf16[256,40,128]{2,0,1:T(8,128)(2,1)}, bf16[256,40,128]{2,0,1:T(8,128)(2,1)}, u32[]{:S(2)}, u32[]{:S(2)}) collective-permute-start(bf16[256,40,128]{2,0,1:T(8,128)(2,1)} %copy.14), channel_id=1, source_target_pairs={{1,0},{2,1},{3,2},{4,3},{5,4},{6,5},{7,6},{8,7},{9,8},{10,9},{11,1... | collective-permute-start | bytes 7864328 | tf_op jit(solution)/shard_map/ppermute | solution.py:21
  977.3 66.0 %collective-permute-start = (bf16[256,40,128]{2,0,1:T(8,128)(2,1)}, bf16[256,40,128]{2,0,1:T(8,128)(2,1)}, u32[]{:S(2)}, u32[]{:S(2)}) collective-permute-start(bf16[256,40,128]{2,0,1:T(8,128)(2,1)} %copy.14), channel_id=1, source_target_pairs={{0,1},{1,2},{2,3},{3,4},{4,5},{5,6},{6,7},{7,8},{8,9},{9,10},{10,1... | collective-permute-start | bytes 7864328 | tf_op jit(solution)/shard_map/ppermute | solution.py:18
  1069.7 9.8 copy-start.6
  1075.2 61.8 %collective-permute-start.2 = (bf16[256,5120]{0,1:T(8,128)(2,1)}, bf16[256,5120]{0,1:T(8,128)(2,1)}, u32[]{:S(2)}, u32[]{:S(2)}) collective-permute-start(bf16[256,5120]{0,1:T(8,128)(2,1)} %fusion.24), channel_id=1, source_target_pairs={{0,128},{128,0},{1,129},{129,1},{2,130},{130,2},{3,131},{131,3},{4... | collective-permute-start | bytes 7864328 | tf_op jit(solution)/shard_map/ppermute | solution.py:29
  1141.1 1.5 copy-start.3
  1150.7 33.3 %collective-permute-start.4 = (bf16[256,40,128]{2,0,1:T(8,128)(2,1)}, bf16[256,40,128]{2,0,1:T(8,128)(2,1)}, u32[]{:S(2)}, u32[]{:S(2)}) collective-permute-start(bf16[256,40,128]{2,0,1:T(8,128)(2,1)} %copy.19), channel_id=1, source_target_pairs={{1,0},{2,1},{3,2},{4,3},{5,4},{6,5},{7,6},{8,7},{9,8},{10,9},{11,1... | collective-permute-start | bytes 7864328 | tf_op jit(solution)/shard_map/ppermute | solution.py:21
  1152.6 32.5 %collective-permute-start.3 = (bf16[256,40,128]{2,0,1:T(8,128)(2,1)}, bf16[256,40,128]{2,0,1:T(8,128)(2,1)}, u32[]{:S(2)}, u32[]{:S(2)}) collective-permute-start(bf16[256,40,128]{2,0,1:T(8,128)(2,1)} %copy.19), channel_id=1, source_target_pairs={{0,1},{1,2},{2,3},{3,4},{4,5},{5,6},{6,7},{7,8},{8,9},{9,10},{10,1... | collective-permute-start | bytes 7864328 | tf_op jit(solution)/shard_map/ppermute | solution.py:18
  1217.1 35.6 %collective-permute-start.5 = (bf16[256,5120]{0,1:T(8,128)(2,1)}, bf16[256,5120]{0,1:T(8,128)(2,1)}, u32[]{:S(2)}, u32[]{:S(2)}) collective-permute-start(bf16[256,5120]{0,1:T(8,128)(2,1)} %fusion.25), channel_id=1, source_target_pairs={{0,128},{128,0},{1,129},{129,1},{2,130},{130,2},{3,131},{131,3},{4... | collective-permute-start | bytes 7864328 | tf_op jit(solution)/shard_map/ppermute | solution.py:29
  1260.6 10.4 copy-start.1
Sparse Core Ops, SparseCore 0:
  20.9 940.6 all-reduce.4
where the time goes:
time: 1280 us
  waiting for transfers between devices  1110 us (87%)
  matrix products  53.1 us (4%)
  other arithmetic  37.4 us (3%)
  local copies, waits for them, and re-layouts  32.4 us (3%)
  between operations  22.6 us (2%)
  starting transfers between devices  20 us (2%)
    unnamed x2, waiting for transfers between devices  930 us
    ppermute x2, waiting for transfers between devices, from_partner(): return lax.ppermute(value, axis, pairs)  89.5 us
    ppermute x2, waiting for transfers between devices, padded(): lax.ppermute(lax.slice_in_dim(block, 0, width, axis=dim), axis, backward)  53.6 us
    ppermute x2, waiting for transfers between devices, padded(): lax.ppermute(lax.slice_in_dim(block, block.shape[dim] - width, None, axis...  39.1 us
    sub x2, matrix products, section(): expo = jnp.exp(scores - top)  26.8 us
    dot_general x2, matrix products, section(): jnp.einsum('hqk,khd->qhd', probs, keys, preferred_element_type=jnp.float32)  26 us
  transfers between devices with their start and end apart: 7, of which 7 were waited for; matrix products, arithmetic and copies ran while one was open for 1% of the time, Pallas kernels for 0%

commit v1 on v0

v1 whole, which is shorter than its diff:
```python
import functools
import math

import jax
import jax.numpy as jnp
from jax import lax
from jax.experimental import pallas as pl
from jax.experimental.pallas import tpu as pltpu
from jax.sharding import PartitionSpec as P

HEADS = 40
HEAD = 128
WINDOW = 128
ROWS = 256
EXT = ROWS + 2 * WINDOW
WIDTH = HEADS * HEAD
PACK = 2
GROUPS = HEADS // PACK
COLS = 120
PLANE = 15
LOG2E = 1.4426950408889634
MASKED = -1e30
MESH = pl.DeviceIdType.MESH
F32 = jnp.float32
BF16 = jnp.bfloat16

LATENT, STALE, FRESH, STATE = range(4)


def features(t_first, t_second, segment):
    shape = (8, HEAD)
    lane = lax.broadcasted_iota(jnp.int32, shape, 1).astype(F32)
    row = lax.broadcasted_iota(jnp.int32, shape, 0)
    freqs = jnp.exp(lane * (-math.log(10000.0) / HEAD))
    angles = jnp.where(row % 2 == 0, t_first, t_second) * freqs
    keep = jnp.where(row // 2 == segment, 1.0, 0.0)
    parts = []
    for value in (jnp.cos(angles), jnp.sin(angles)):
        parts.append(value / (1.0 + jnp.exp(-value)) * keep)
    return jnp.concatenate(parts, axis=1).astype(BF16)


def kernel(
    latent_hbm,
    stale_hbm,
    step_ids,
    sigma_table,
    weight,
    latent_out,
    hidden_out,
    x,
    out,
    rstd,
    offset,
    bias,
    keys,
    msg_out,
    msg_in,
    plane,
    mods,
    load_sem,
    out_sem,
    recv_on,
    recv_off,
    send_on,
    send_off,
    recv_msg,
    send_msg,
    recv_mod1,
    send_mod1,
    recv_mod2,
    send_mod2,
    recv_mod3,
    send_mod3,
):
    seg = lax.axis_index("segment")
    seq = lax.axis_index("seq")
    core = seq % 2
    spot = seq % 4
    across = (seq // 4) % 4
    deep = seq // 16
    quad = seg * 4 + spot
    last = 127
    on_chip = seq + 1 - 2 * core
    off_chip = (seq + 127 + 2 * core) % 128

    src_on = pl.multiple_of(256 - 128 * core, 128)
    src_off = pl.multiple_of(128 + 128 * core, 128)
    dst_on = pl.multiple_of(384 * core, 128)
    dst_off = pl.multiple_of(384 - 384 * core, 128)

    def peer_quad(k):
        other = (quad + k) % 8
        return (other // 4, seq - spot + other % 4)

    def peer_across(k):
        return (seg, seq - across * 4 + (across + k) % 4 * 4)

    def peer_deep(k):
        return (seg, (seq + 16 * k) % 128)

    for arr, source in ((LATENT, latent_hbm), (STALE, stale_hbm)):

        @pl.loop(0, HEADS)
        def _(h, arr=arr, source=source):
            cols = pl.ds(pl.multiple_of(h * HEAD, HEAD), HEAD)
            pltpu.make_async_copy(
                source.at[:, cols], x.at[arr, h, pl.ds(WINDOW, ROWS)], load_sem.at[arr]
            ).start()

    def wait_load(arr):
        whole = x.at[arr, :, pl.ds(WINDOW, ROWS)]
        pltpu.make_async_copy(whole, whole, load_sem.at[arr]).wait()

    barrier = pltpu.get_barrier_semaphore()
    partners = [peer_quad(k) for k in range(1, 8)]
    partners += [peer_across(k) for k in range(1, 4)]
    partners += [peer_deep(k) for k in range(1, 8)]
    partners += [(0, off_chip), (1, off_chip)]
    for partner in partners:
        pl.semaphore_signal(barrier, inc=1, device_id=partner, device_id_type=MESH)

    times = [sigma_table[step_ids[i]].astype(F32) for i in range(3)]
    feats = features(times[0], times[1], seg)
    columns = jnp.dot(feats, weight[0], preferred_element_type=F32)
    plane[across, quad] = jnp.concatenate([columns, jnp.zeros((8, HEAD - COLS), F32)], axis=1)
    rates = [(times[i + 1] - times[i]) * F32(1.0 / 1000.0) for i in range(2)]

    pl.semaphore_wait(barrier, len(partners))

    def mod1(k):
        ref = plane.at[across, quad]
        return pltpu.make_async_remote_copy(
            ref, ref, send_mod1.at[k], recv_mod1.at[k], peer_quad(k), MESH
        )

    def mod2(k):
        ref = plane.at[across]
        return pltpu.make_async_remote_copy(
            ref, ref, send_mod2.at[k], recv_mod2.at[k], peer_across(k), MESH
        )

    def mod3(k):
        ref = mods.at[pl.ds(deep * PLANE, PLANE)]
        return pltpu.make_async_remote_copy(
            ref, ref, send_mod3.at[k], recv_mod3.at[k], peer_deep(k), MESH
        )

    def halo_on(arr, g):
        heads = pl.ds(g * PACK, PACK)
        return pltpu.make_async_remote_copy(
            x.at[arr, heads, pl.ds(src_on, WINDOW)],
            x.at[arr, heads, pl.ds(dst_on, WINDOW)],
            send_on.at[arr],
            recv_on.at[arr, g],
            (seg, on_chip),
            MESH,
        )

    def halo_off(arr, g, to):
        heads = pl.ds(g * PACK, PACK)
        return pltpu.make_async_remote_copy(
            x.at[arr, heads, pl.ds(src_off, WINDOW)],
            x.at[arr, heads, pl.ds(dst_off, WINDOW)],
            send_off.at[arr],
            recv_off.at[arr, g],
            (to, off_chip),
            MESH,
        )

    def send_halo(arr, g):
        halo_on(arr, g).start()

        @pl.when(g % 2 == seg)
        def _():
            halo_off(arr, g, 0).start()
            halo_off(arr, g, 1).start()

    def send_all(arr):
        @pl.loop(0, GROUPS)
        def _(g):
            send_halo(arr, g)

    def message(arr, side):
        return pltpu.make_async_remote_copy(
            msg_out.at[arr, side],
            msg_in.at[arr, side],
            send_msg.at[arr, side],
            recv_msg.at[arr, side],
            (seg, on_chip if side == 0 else off_chip),
            MESH,
        )

    def own_stats(arr):
        own = pl.ds(WINDOW, ROWS)

        def add(h, total):
            return total + x[arr, h, own].astype(F32)

        total = lax.fori_loop(0, HEADS, add, jnp.zeros((ROWS, HEAD), F32))
        mean = jnp.sum(total, axis=1, keepdims=True) * F32(1.0 / WIDTH)
        mean = jnp.broadcast_to(mean, (ROWS, HEAD))
        offset[arr, own] = mean

        def add_square(h, total):
            part = x[arr, h, own].astype(F32) - offset[arr, own]
            return total + part * part

        total = lax.fori_loop(0, HEADS, add_square, jnp.zeros((ROWS, HEAD), F32))
        var = jnp.sum(total, axis=1, keepdims=True) * F32(1.0 / WIDTH)
        scale = jnp.broadcast_to(lax.rsqrt(var + 1e-06), (ROWS, HEAD))
        rstd[arr, own] = scale
        offset[arr, own] = -mean * scale
        row = lax.broadcasted_iota(jnp.int32, (8, HEAD), 0)
        for side, start in ((0, src_on), (1, src_off)):
            first = rstd[arr, pl.ds(start, WINDOW)].T[:8]
            second = offset[arr, pl.ds(start, WINDOW)].T[:8]
            msg_out[arr, side] = jnp.where(row == 0, first, second)
            message(arr, side).start()

    def halo_stats(arr):
        for side, start in ((0, dst_off), (1, dst_on)):
            message(arr, side).wait_recv()
            rows = pl.ds(start, WINDOW)
            got = msg_in[arr, side]
            rstd[arr, rows] = jnp.broadcast_to(got[0:1], (WINDOW, HEAD)).T
            offset[arr, rows] = jnp.broadcast_to(got[1:2], (WINDOW, HEAD)).T

    def rows_of(low):
        return pl.ds(low + WINDOW, WINDOW)

    def run_section(arr, mod_row, finish, after):
        @pl.loop(0, GROUPS)
        def _(g):
            halo_on(arr, g).wait_recv()
            halo_off(arr, g, seg).wait_recv()
            for u in range(PACK):
                h = g * PACK + u
                one_head(arr, mod_row, h, u, finish)
            after(g)

    def one_head(arr, mod_row, h, u, finish):
        shift = mods[h][mod_row : mod_row + 1]
        scale = mods[HEADS + h][mod_row : mod_row + 1] + 1.0
        gate = mods[2 * HEADS + h][mod_row : mod_row + 1]
        raw = x[arr, h].astype(F32)
        normed = (raw * rstd[arr] + offset[arr]) * scale + shift
        keys[u, :, :HEAD] = normed.astype(BF16)
        for b in range(2):
            low = b * WINDOW
            query = keys[u, low + WINDOW : low + 2 * WINDOW, :HEAD]
            span = keys[u, low : low + 3 * WINDOW]
            scores = lax.dot_general(
                query, span[:, :HEAD], (((1,), (1,)), ((), ())), preferred_element_type=F32
            )
            scores = scores * F32(LOG2E / HEAD)
            left = scores[:, :WINDOW] + bias[2 * b]
            mid = scores[:, WINDOW : 2 * WINDOW]
            right = scores[:, 2 * WINDOW :] + bias[2 * b + 1]
            top = jnp.max(jnp.maximum(jnp.maximum(left, right), mid), axis=1, keepdims=True)
            expo = jnp.concatenate(
                [jnp.exp2(part - top).astype(BF16) for part in (left, mid, right)], axis=1
            )
            both = jnp.dot(expo, span, preferred_element_type=F32)
            attn = both[:, :HEAD] / both[:, HEAD:]
            own = x[arr, h, rows_of(low)].astype(F32)
            finish(h, low, own + gate * attn)

    for k in range(1, 8):
        mod1(k).start()
    wait_load(LATENT)
    send_all(LATENT)
    for k in range(1, 8):
        mod1(k).wait_recv()
    for k in range(1, 4):
        mod2(k).start()

    keys[:, :, HEAD:] = jnp.ones((PACK, EXT, HEAD), BF16)
    query_at = lax.broadcasted_iota(jnp.int32, (WINDOW, WINDOW), 0)
    key_at = lax.broadcasted_iota(jnp.int32, (WINDOW, WINDOW), 1)
    left_bias = jnp.where(key_at >= query_at, 0.0, MASKED)
    right_bias = jnp.where(key_at <= query_at, 0.0, MASKED)
    bias[0] = jnp.where(seq == 0, MASKED, left_bias)
    bias[1] = right_bias
    bias[2] = left_bias
    bias[3] = jnp.where(seq == last, MASKED, right_bias)
    own_stats(LATENT)

    for k in range(1, 4):
        mod2(k).wait_recv()
    lane = lax.broadcasted_iota(jnp.int32, (8, HEAD), 1)

    def chunk(k):
        return plane[k // 4, k % 4] + plane[k // 4, 4 + k % 4]

    for k in range(PLANE):
        first, second = chunk(k), chunk(k + 1)
        if k > 0:
            first = pltpu.roll(first, HEAD - 8 * k, 1)
        second = pltpu.roll(second, COLS - 8 * k, 1)
        row = jnp.where(lane < COLS - 8 * k, first, second)
        mods[deep * PLANE + k] = row[:4]
    for k in range(1, 8):
        mod3(k).start()

    wait_load(STALE)
    send_all(STALE)
    own_stats(STALE)
    for k in range(1, 8):
        mod3(k).wait_recv()

    def to_fresh(h, low, value):
        x[FRESH, h, rows_of(low)] = value.astype(BF16)

    def to_state(h, low, value):
        now = x[LATENT, h, rows_of(low)].astype(F32)
        x[STATE, h, rows_of(low)] = (now + rates[0] * value).astype(BF16)

    def to_latent_out(h, low, value):
        now = x[STATE, h, rows_of(low)].astype(F32)
        out[0, h, low : low + WINDOW] = (now + rates[1] * value).astype(BF16)

    def to_hidden_out(h, low, value):
        out[1, h, low : low + WINDOW] = value.astype(BF16)

    def write(which, target):
        def after(g):
            for u in range(PACK):
                h = g * PACK + u
                cols = pl.ds(pl.multiple_of(h * HEAD, HEAD), HEAD)
                pltpu.make_async_copy(out.at[which, h], target.at[:, cols], out_sem.at[which]).start()

        return after

    halo_stats(LATENT)
    run_section(LATENT, 0, to_fresh, functools.partial(send_halo, FRESH))
    own_stats(FRESH)
    halo_stats(STALE)
    run_section(STALE, 2, to_state, functools.partial(send_halo, STATE))
    own_stats(STATE)
    halo_stats(FRESH)
    run_section(FRESH, 3, to_latent_out, write(0, latent_out))
    halo_stats(STATE)
    run_section(STATE, 1, to_hidden_out, write(1, hidden_out))

    for which in range(2):
        pltpu.make_async_copy(out.at[which], out.at[which], out_sem.at[which]).wait()
    for k in range(1, 8):
        mod1(k).wait_send()
        mod3(k).wait_send()
    for k in range(1, 4):
        mod2(k).wait_send()
    for arr in range(4):
        for side in range(2):
            message(arr, side).wait_send()
        sent = x.at[arr, :, pl.ds(0, WINDOW)]
        pltpu.make_async_copy(sent, sent, send_on.at[arr]).wait()
        pltpu.make_async_copy(sent, sent, send_off.at[arr]).wait()


def per_device(latent, stale_hidden, step_ids, sigma_table, mod_weight):
    dma = pltpu.SemaphoreType.DMA
    anywhere = pl.BlockSpec(memory_space=pl.ANY)
    scalars = pl.BlockSpec(memory_space=pltpu.SMEM)
    result = jax.ShapeDtypeStruct(latent.shape, latent.dtype)
    return pl.pallas_call(
        kernel,
        out_shape=(result, result),
        in_specs=[anywhere, anywhere, scalars, scalars, pl.BlockSpec(memory_space=pltpu.VMEM)],
        out_specs=(anywhere, anywhere),
        scratch_shapes=[
            pltpu.VMEM((4, HEADS, EXT, HEAD), BF16),
            pltpu.VMEM((2, HEADS, ROWS, HEAD), BF16),
            pltpu.VMEM((4, EXT, HEAD), F32),
            pltpu.VMEM((4, EXT, HEAD), F32),
            pltpu.VMEM((4, WINDOW, WINDOW), F32),
            pltpu.VMEM((PACK, EXT, 2 * HEAD), BF16),
            pltpu.VMEM((4, 2, 8, HEAD), F32),
            pltpu.VMEM((4, 2, 8, HEAD), F32),
            pltpu.VMEM((4, 8, 8, HEAD), F32),
            pltpu.VMEM((3 * HEADS, 4, HEAD), F32),
            dma((2,)),
            dma((2,)),
            dma((4, GROUPS)),
            dma((4, GROUPS)),
            dma((4,)),
            dma((4,)),
            dma((4, 2)),
            dma((4, 2)),
            dma((8,)),
            dma((8,)),
            dma((4,)),
            dma((4,)),
            dma((8,)),
            dma((8,)),
        ],
        compiler_params=pltpu.CompilerParams(
            collective_id=0, has_side_effects=True, vmem_limit_bytes=48 * 1024 * 1024
        ),
    )(latent, stale_hidden, step_ids, sigma_table, mod_weight)


def solution(mesh):
    placed = (P("seq", None), P("seq", None), P(), P(), P("segment", None, "seq"))
    return jax.shard_map(
        per_device,
        mesh=mesh,
        in_specs=placed,
        out_specs=(P("seq", None), P("seq", None)),
        check_vma=False,
    )
```

time: 1280 us -> 106 us (0.08)
  the two profiles are of different devices: /device:TPU:1 before, /device:TPU:32 now
where the time goes in v1:
time: 106 us; the launch traced here: 105 us
  Pallas kernels  98.8 us (93%)
  local copies, waits for them, and re-layouts  5.27 us (5%)
    pallas_call x1, Pallas kernels, per_device(): pl.pallas_call(kernel, out_shape=(result, result), in_specs=[anywhere, an...  98.8 us
    unnamed x7, local copies, waits for them, and re-layouts  5.27 us

profile of v1, /device:TPU:32, one launch (start us, length us, event | category | flops | bytes accessed | tf_op | source)
XLA Modules:
  0.0 104.7 jit_solution(16566013213459216663)
XLA Ops:
  0.6 0.9 copy.7.weight
  1.6 0.0 copy-start
  1.6 0.7 copy-done
  2.3 0.0 copy-start.1
  2.3 0.7 copy-done.1
  2.9 98.8 %shard_map.68 = (bf16[256,5120]{1,0:T(8,128)(2,1)S(1)}, bf16[256,5120]{1,0:T(8,128)(2,1)S(1)}) custom-call(bf16[256,5120]{1,0:T(8,128)(2,1)} %latent_hbm.1, bf16[256,5120]{1,0:T(8,128)(2,1)} %stale_hbm.1, s32[3]{0:T(128)S(1)} %copy-done.1, s32[1000]{0:T(1024)S(1)} %copy-done, bf16[1,256,120]{2,1,0:T(8,128)(2,1)S(1)} %copy.7.weight), custom_call_target="tpu_custom_call" | custom-call | tf_op jit(solution)/shard_map/pallas_call | solution.py:366
  101.7 1.5 %copy.10 = bf16[256,5120]{1,0:T(8,128)(2,1)} copy(bf16[256,5120]{1,0:T(8,128)(2,1)S(1)} %get-tuple-element.4) | data formatting | bytes 5242880
  103.2 1.5 %copy.11 = bf16[256,5120]{1,0:T(8,128)(2,1)} copy(bf16[256,5120]{1,0:T(8,128)(2,1)S(1)} %get-tuple-element.5) | data formatting | bytes 5242880
Async XLA Ops:
  1.6 0.7 copy-start
  2.3 0.7 copy-start.1

commit v2 on v1

--- a/solution.py
+++ b/solution.py
@@ -14,11 +14,11 @@
 ROWS = 256
 EXT = ROWS + 2 * WINDOW
 WIDTH = HEADS * HEAD
-PACK = 2
+PACK = 8
 GROUPS = HEADS // PACK
 COLS = 120
 PLANE = 15
-LOG2E = 1.4426950408889634
+ROOT = math.sqrt(math.log2(math.e) / HEAD)
 MASKED = -1e30
 MESH = pl.DeviceIdType.MESH
 F32 = jnp.float32
@@ -48,8 +48,12 @@
     weight,
     latent_out,
     hidden_out,
-    x,
-    out,
+    x_latent,
+    x_stale,
+    x_fresh,
+    x_state,
+    out_latent,
+    out_hidden,
     rstd,
     offset,
     bias,
@@ -73,6 +77,8 @@
     recv_mod3,
     send_mod3,
 ):
+    x = (x_latent, x_stale, x_fresh, x_state)
+    out = (out_latent, out_hidden)
     seg = lax.axis_index("segment")
     seq = lax.axis_index("seq")
     core = seq % 2
@@ -105,11 +111,11 @@
         def _(h, arr=arr, source=source):
             cols = pl.ds(pl.multiple_of(h * HEAD, HEAD), HEAD)
             pltpu.make_async_copy(
-                source.at[:, cols], x.at[arr, h, pl.ds(WINDOW, ROWS)], load_sem.at[arr]
+                source.at[:, cols], x[arr].at[h, pl.ds(WINDOW, ROWS)], load_sem.at[arr]
             ).start()
 
     def wait_load(arr):
-        whole = x.at[arr, :, pl.ds(WINDOW, ROWS)]
+        whole = x[arr].at[:, pl.ds(WINDOW, ROWS)]
         pltpu.make_async_copy(whole, whole, load_sem.at[arr]).wait()
 
     barrier = pltpu.get_barrier_semaphore()
@@ -149,32 +155,29 @@
     def halo_on(arr, g):
         heads = pl.ds(g * PACK, PACK)
         return pltpu.make_async_remote_copy(
-            x.at[arr, heads, pl.ds(src_on, WINDOW)],
-            x.at[arr, heads, pl.ds(dst_on, WINDOW)],
+            x[arr].at[heads, pl.ds(src_on, WINDOW)],
+            x[arr].at[heads, pl.ds(dst_on, WINDOW)],
             send_on.at[arr],
             recv_on.at[arr, g],
             (seg, on_chip),
             MESH,
         )
 
-    def halo_off(arr, g, to):
-        heads = pl.ds(g * PACK, PACK)
-        return pltpu.make_async_remote_copy(
-            x.at[arr, heads, pl.ds(src_off, WINDOW)],
-            x.at[arr, heads, pl.ds(dst_off, WINDOW)],
+    def halo_off(arr, g, half, to):
+        heads = pl.ds(g * PACK + half * (PACK // 2), PACK // 2)
+        return pltpu.make_async_remote_copy(
+            x[arr].at[heads, pl.ds(src_off, WINDOW)],
+            x[arr].at[heads, pl.ds(dst_off, WINDOW)],
             send_off.at[arr],
-            recv_off.at[arr, g],
+            recv_off.at[arr, 2 * g + half],
             (to, off_chip),
             MESH,
         )
 
     def send_halo(arr, g):
         halo_on(arr, g).start()
-
-        @pl.when(g % 2 == seg)
-        def _():
-            halo_off(arr, g, 0).start()
-            halo_off(arr, g, 1).start()
+        halo_off(arr, g, seg, 0).start()
+        halo_off(arr, g, seg, 1).start()
 
     def send_all(arr):
         @pl.loop(0, GROUPS)
@@ -195,18 +198,18 @@
         own = pl.ds(WINDOW, ROWS)
 
         def add(h, total):
-            return total + x[arr, h, own].astype(F32)
-
-        total = lax.fori_loop(0, HEADS, add, jnp.zeros((ROWS, HEAD), F32))
+            return total + x[arr][h, own].astype(F32)
+
+        total = lax.fori_loop(0, HEADS, add, jnp.zeros((ROWS, HEAD), F32), unroll=4)
         mean = jnp.sum(total, axis=1, keepdims=True) * F32(1.0 / WIDTH)
         mean = jnp.broadcast_to(mean, (ROWS, HEAD))
         offset[arr, own] = mean
 
         def add_square(h, total):
-            part = x[arr, h, own].astype(F32) - offset[arr, own]
+            part = x[arr][h, own].astype(F32) - offset[arr, own]
             return total + part * part
 
-        total = lax.fori_loop(0, HEADS, add_square, jnp.zeros((ROWS, HEAD), F32))
+        total = lax.fori_loop(0, HEADS, add_square, jnp.zeros((ROWS, HEAD), F32), unroll=4)
         var = jnp.sum(total, axis=1, keepdims=True) * F32(1.0 / WIDTH)
         scale = jnp.broadcast_to(lax.rsqrt(var + 1e-06), (ROWS, HEAD))
         rstd[arr, own] = scale
@@ -226,45 +229,52 @@
             rstd[arr, rows] = jnp.broadcast_to(got[0:1], (WINDOW, HEAD)).T
             offset[arr, rows] = jnp.broadcast_to(got[1:2], (WINDOW, HEAD)).T
 
-    def rows_of(low):
-        return pl.ds(low + WINDOW, WINDOW)
-
     def run_section(arr, mod_row, finish, after):
         @pl.loop(0, GROUPS)
         def _(g):
             halo_on(arr, g).wait_recv()
-            halo_off(arr, g, seg).wait_recv()
-            for u in range(PACK):
-                h = g * PACK + u
-                one_head(arr, mod_row, h, u, finish)
+            halo_off(arr, g, 0, seg).wait_recv()
+            halo_off(arr, g, 1, seg).wait_recv()
+            heads = [g * PACK + u for u in range(PACK)]
+            for u, h in enumerate(heads):
+                shift = mods[h][mod_row : mod_row + 1]
+                scale = mods[HEADS + h][mod_row : mod_row + 1]
+                raw = x[arr][h].astype(F32)
+                normed = (raw * rstd[arr] + offset[arr]) * scale + shift
+                keys[u, :, :HEAD] = normed.astype(BF16)
+            results = []
+            for u, h in enumerate(heads):
+                gate = mods[2 * HEADS + h][mod_row : mod_row + 1]
+                attn = attend(u)
+                for b in range(2):
+                    own = x[arr][h, rows_of(b)].astype(F32)
+                    part = attn[b * WINDOW : (b + 1) * WINDOW]
+                    results.append((h, b, own + gate * part))
+            finish(results)
             after(g)
 
-    def one_head(arr, mod_row, h, u, finish):
-        shift = mods[h][mod_row : mod_row + 1]
-        scale = mods[HEADS + h][mod_row : mod_row + 1] + 1.0
-        gate = mods[2 * HEADS + h][mod_row : mod_row + 1]
-        raw = x[arr, h].astype(F32)
-        normed = (raw * rstd[arr] + offset[arr]) * scale + shift
-        keys[u, :, :HEAD] = normed.astype(BF16)
+    def attend(u):
+        scores = lax.dot_general(
+            keys[u, WINDOW : WINDOW + ROWS, :HEAD],
+            keys[u, :, :HEAD],
+            (((1,), (1,)), ((), ())),
+            preferred_element_type=F32,
+        )
+        blocks = []
+        none = jnp.zeros((WINDOW, WINDOW), BF16)
         for b in range(2):
-            low = b * WINDOW
-            query = keys[u, low + WINDOW : low + 2 * WINDOW, :HEAD]
-            span = keys[u, low : low + 3 * WINDOW]
-            scores = lax.dot_general(
-                query, span[:, :HEAD], (((1,), (1,)), ((), ())), preferred_element_type=F32
-            )
-            scores = scores * F32(LOG2E / HEAD)
-            left = scores[:, :WINDOW] + bias[2 * b]
-            mid = scores[:, WINDOW : 2 * WINDOW]
-            right = scores[:, 2 * WINDOW :] + bias[2 * b + 1]
+            rows = scores[b * WINDOW : (b + 1) * WINDOW, b * WINDOW : (b + 3) * WINDOW]
+            left = rows[:, :WINDOW] + bias[2 * b]
+            mid = rows[:, WINDOW : 2 * WINDOW]
+            right = rows[:, 2 * WINDOW :] + bias[2 * b + 1]
             top = jnp.max(jnp.maximum(jnp.maximum(left, right), mid), axis=1, keepdims=True)
-            expo = jnp.concatenate(
-                [jnp.exp2(part - top).astype(BF16) for part in (left, mid, right)], axis=1
-            )
-            both = jnp.dot(expo, span, preferred_element_type=F32)
-            attn = both[:, :HEAD] / both[:, HEAD:]
-            own = x[arr, h, rows_of(low)].astype(F32)
-            finish(h, low, own + gate * attn)
+            expo = [jnp.exp2(part - top).astype(BF16) for part in (left, mid, right)]
+            blocks.append(jnp.concatenate([none] * b + expo + [none] * (1 - b), axis=1))
+        both = jnp.dot(jnp.concatenate(blocks, axis=0), keys[u], preferred_element_type=F32)
+        return both[:, :HEAD] * pl.reciprocal(both[:, HEAD:], approx=True)
+
+    def rows_of(b):
+        return pl.ds(b * WINDOW + WINDOW, WINDOW)
 
     for k in range(1, 8):
         mod1(k).start()
@@ -299,7 +309,10 @@
             first = pltpu.roll(first, HEAD - 8 * k, 1)
         second = pltpu.roll(second, COLS - 8 * k, 1)
         row = jnp.where(lane < COLS - 8 * k, first, second)
-        mods[deep * PLANE + k] = row[:4]
+        at = deep * PLANE + k
+        factor = jnp.where(at < 2 * HEADS, F32(ROOT), F32(1.0 / ROOT))
+        row = (row + jnp.where(at // HEADS == 1, F32(1.0), F32(0.0))) * factor
+        mods[at] = row[:4]
     for k in range(1, 8):
         mod3(k).start()
 
@@ -309,26 +322,30 @@
     for k in range(1, 8):
         mod3(k).wait_recv()
 
-    def to_fresh(h, low, value):
-        x[FRESH, h, rows_of(low)] = value.astype(BF16)
-
-    def to_state(h, low, value):
-        now = x[LATENT, h, rows_of(low)].astype(F32)
-        x[STATE, h, rows_of(low)] = (now + rates[0] * value).astype(BF16)
-
-    def to_latent_out(h, low, value):
-        now = x[STATE, h, rows_of(low)].astype(F32)
-        out[0, h, low : low + WINDOW] = (now + rates[1] * value).astype(BF16)
-
-    def to_hidden_out(h, low, value):
-        out[1, h, low : low + WINDOW] = value.astype(BF16)
+    def to_fresh(results):
+        for h, b, value in results:
+            x[FRESH][h, rows_of(b)] = value.astype(BF16)
+
+    def to_state(results):
+        now = [x[LATENT][h, rows_of(b)].astype(F32) for h, b, _ in results]
+        for (h, b, value), base in zip(results, now):
+            x[STATE][h, rows_of(b)] = (base + rates[0] * value).astype(BF16)
+
+    def to_latent_out(results):
+        now = [x[STATE][h, rows_of(b)].astype(F32) for h, b, _ in results]
+        for (h, b, value), base in zip(results, now):
+            out[0][h, b * WINDOW : (b + 1) * WINDOW] = (base + rates[1] * value).astype(BF16)
+
+    def to_hidden_out(results):
+        for h, b, value in results:
+            out[1][h, b * WINDOW : (b + 1) * WINDOW] = value.astype(BF16)
 
     def write(which, target):
         def after(g):
             for u in range(PACK):
                 h = g * PACK + u
                 cols = pl.ds(pl.multiple_of(h * HEAD, HEAD), HEAD)
-                pltpu.make_async_copy(out.at[which, h], target.at[:, cols], out_sem.at[which]).start()
+                pltpu.make_async_copy(out[which].at[h], target.at[:, cols], out_sem.at[which]).start()
 
         return after
 
@@ -344,7 +361,7 @@
     run_section(STATE, 1, to_hidden_out, write(1, hidden_out))
 
     for which in range(2):
-        pltpu.make_async_copy(out.at[which], out.at[which], out_sem.at[which]).wait()
+        pltpu.make_async_copy(out[which], out[which], out_sem.at[which]).wait()
     for k in range(1, 8):
         mod1(k).wait_send()
         mod3(k).wait_send()
@@ -353,7 +370,7 @@
     for arr in range(4):
         for side in range(2):
             message(arr, side).wait_send()
-        sent = x.at[arr, :, pl.ds(0, WINDOW)]
+        sent = x[arr].at[:, pl.ds(0, WINDOW)]
         pltpu.make_async_copy(sent, sent, send_on.at[arr]).wait()
         pltpu.make_async_copy(sent, sent, send_off.at[arr]).wait()
 
@@ -369,8 +386,8 @@
         in_specs=[anywhere, anywhere, scalars, scalars, pl.BlockSpec(memory_space=pltpu.VMEM)],
         out_specs=(anywhere, anywhere),
         scratch_shapes=[
-            pltpu.VMEM((4, HEADS, EXT, HEAD), BF16),
-            pltpu.VMEM((2, HEADS, ROWS, HEAD), BF16),
+            *[pltpu.VMEM((HEADS, EXT, HEAD), BF16)] * 4,
+            *[pltpu.VMEM((HEADS, ROWS, HEAD), BF16)] * 2,
             pltpu.VMEM((4, EXT, HEAD), F32),
             pltpu.VMEM((4, EXT, HEAD), F32),
             pltpu.VMEM((4, WINDOW, WINDOW), F32),
@@ -382,7 +399,7 @@
             dma((2,)),
             dma((2,)),
             dma((4, GROUPS)),
-            dma((4, GROUPS)),
+            dma((4, 2 * GROUPS)),
             dma((4,)),
             dma((4,)),
             dma((4, 2)),

time: 106 us -> 91.5 us (0.86)
  Pallas kernels: 98.8 us -> 84.9 us
    pallas_call x1, Pallas kernels: 98.8 us -> 84.9 us  [per_device(): pl.pallas_call(kernel, out_shape=(result, result), in_specs=[anywhere, an...]
where the time goes in v2:
time: 91.5 us; the launch traced here: 90.8 us
  Pallas kernels  84.9 us (93%)
  local copies, waits for them, and re-layouts  5.27 us (6%)
    pallas_call x1, Pallas kernels, per_device(): pl.pallas_call(kernel, out_shape=(result, result), in_specs=[anywhere, an...  84.9 us
    unnamed x7, local copies, waits for them, and re-layouts  5.27 us

profile of v2, /device:TPU:32, one launch (start us, length us, event | category | flops | bytes accessed | tf_op | source)
XLA Modules:
  0.0 90.8 jit_solution(14420736340868886223)
XLA Ops:
  0.6 0.9 %copy.7.weight = bf16[1,256,120]{2,1,0:T(8,128)(2,1)S(1)} copy(bf16[1,256,120]{1,2,0:T(8,128)(2,1)} %param.9) | data formatting | bytes 122880 | tf_op args[4]
  1.6 0.0 copy-start
  1.6 0.7 copy-done
  2.3 0.0 copy-start.1
  2.3 0.7 copy-done.1
  2.9 84.9 %shard_map.68 = (bf16[256,5120]{1,0:T(8,128)(2,1)S(1)}, bf16[256,5120]{1,0:T(8,128)(2,1)S(1)}) custom-call(bf16[256,5120]{1,0:T(8,128)(2,1)} %latent_hbm.1, bf16[256,5120]{1,0:T(8,128)(2,1)} %stale_hbm.1, s32[3]{0:T(128)S(1)} %copy-done.1, s32[1000]{0:T(1024)S(1)} %copy-done, bf16[1,256,120]{2,1,0:T(8,128)(2,1)S(1)} %copy.7.weight), custom_call_target="tpu_custom_call" | custom-call | tf_op jit(solution)/shard_map/pallas_call | solution.py:383
  87.8 1.5 %copy.10 = bf16[256,5120]{1,0:T(8,128)(2,1)} copy(bf16[256,5120]{1,0:T(8,128)(2,1)S(1)} %get-tuple-element.4) | data formatting | bytes 5242880
  89.3 1.5 %copy.11 = bf16[256,5120]{1,0:T(8,128)(2,1)} copy(bf16[256,5120]{1,0:T(8,128)(2,1)S(1)} %get-tuple-element.5) | data formatting | bytes 5242880
Async XLA Ops:
  1.6 0.7 copy-start
  2.3 0.7 copy-start.1

commit v3 on v2

--- a/solution.py
+++ b/solution.py
@@ -1,4 +1,3 @@
-import functools
 import math
 
 import jax
@@ -18,6 +17,7 @@
 GROUPS = HEADS // PACK
 COLS = 120
 PLANE = 15
+EARLY = 2
 ROOT = math.sqrt(math.log2(math.e) / HEAD)
 MASKED = -1e30
 MESH = pl.DeviceIdType.MESH
@@ -61,6 +61,7 @@
     msg_out,
     msg_in,
     plane,
+    joint,
     mods,
     load_sem,
     out_sem,
@@ -76,6 +77,8 @@
     send_mod2,
     recv_mod3,
     send_mod3,
+    from_below,
+    from_above,
 ):
     x = (x_latent, x_stale, x_fresh, x_state)
     out = (out_latent, out_hidden)
@@ -105,10 +108,9 @@
     def peer_deep(k):
         return (seg, (seq + 16 * k) % 128)
 
-    for arr, source in ((LATENT, latent_hbm), (STALE, stale_hbm)):
-
+    def load(arr, source):
         @pl.loop(0, HEADS)
-        def _(h, arr=arr, source=source):
+        def _(h):
             cols = pl.ds(pl.multiple_of(h * HEAD, HEAD), HEAD)
             pltpu.make_async_copy(
                 source.at[:, cols], x[arr].at[h, pl.ds(WINDOW, ROWS)], load_sem.at[arr]
@@ -118,30 +120,52 @@
         whole = x[arr].at[:, pl.ds(WINDOW, ROWS)]
         pltpu.make_async_copy(whole, whole, load_sem.at[arr]).wait()
 
+    inner = (seq > 0) & (seq < last)
+    above, below = peer_deep(1), peer_deep(7)
     barrier = pltpu.get_barrier_semaphore()
+
+    @pl.when(inner)
+    def _():
+        for to in range(2):
+            pl.semaphore_signal(barrier, inc=1, device_id=(to, off_chip), device_id_type=MESH)
+
     partners = [peer_quad(k) for k in range(1, 8)]
     partners += [peer_across(k) for k in range(1, 4)]
-    partners += [peer_deep(k) for k in range(1, 8)]
-    partners += [(0, off_chip), (1, off_chip)]
+    partners += [above, below]
     for partner in partners:
         pl.semaphore_signal(barrier, inc=1, device_id=partner, device_id_type=MESH)
+    load(LATENT, latent_hbm)
 
     times = [sigma_table[step_ids[i]].astype(F32) for i in range(3)]
     feats = features(times[0], times[1], seg)
-    columns = jnp.dot(feats, weight[0], preferred_element_type=F32)
-    plane[across, quad] = jnp.concatenate([columns, jnp.zeros((8, HEAD - COLS), F32)], axis=1)
+    columns = lax.dot_general(
+        feats, weight[0], (((1,), (1,)), ((), ())), preferred_element_type=F32
+    )
+    plane[quad] = jnp.concatenate([columns, jnp.zeros((8, HEAD - COLS), F32)], axis=1)
     rates = [(times[i + 1] - times[i]) * F32(1.0 / 1000.0) for i in range(2)]
 
-    pl.semaphore_wait(barrier, len(partners))
+    @pl.when(inner)
+    def _():
+        pl.semaphore_wait(barrier, len(partners) + 2)
+
+    @pl.when(jnp.logical_not(inner))
+    def _():
+        pl.semaphore_wait(barrier, len(partners))
+
+    def tell(up, down):
+        if up:
+            pl.semaphore_signal(from_below, inc=1, device_id=above, device_id_type=MESH)
+        if down:
+            pl.semaphore_signal(from_above, inc=1, device_id=below, device_id_type=MESH)
 
     def mod1(k):
-        ref = plane.at[across, quad]
+        ref = plane.at[quad]
         return pltpu.make_async_remote_copy(
             ref, ref, send_mod1.at[k], recv_mod1.at[k], peer_quad(k), MESH
         )
 
     def mod2(k):
-        ref = plane.at[across]
+        ref = joint.at[across]
         return pltpu.make_async_remote_copy(
             ref, ref, send_mod2.at[k], recv_mod2.at[k], peer_across(k), MESH
         )
@@ -176,11 +200,14 @@
 
     def send_halo(arr, g):
         halo_on(arr, g).start()
-        halo_off(arr, g, seg, 0).start()
-        halo_off(arr, g, seg, 1).start()
-
-    def send_all(arr):
-        @pl.loop(0, GROUPS)
+
+        @pl.when(inner)
+        def _():
+            halo_off(arr, g, seg, 0).start()
+            halo_off(arr, g, seg, 1).start()
+
+    def send_groups(arr, first, end):
+        @pl.loop(first, end)
         def _(g):
             send_halo(arr, g)
 
@@ -193,6 +220,12 @@
             (seg, on_chip if side == 0 else off_chip),
             MESH,
         )
+
+    def each_side(side, act):
+        if side == 0:
+            act()
+        else:
+            pl.when(inner)(act)
 
     def own_stats(arr):
         own = pl.ds(WINDOW, ROWS)
@@ -219,11 +252,11 @@
             first = rstd[arr, pl.ds(start, WINDOW)].T[:8]
             second = offset[arr, pl.ds(start, WINDOW)].T[:8]
             msg_out[arr, side] = jnp.where(row == 0, first, second)
-            message(arr, side).start()
+            each_side(side, lambda side=side: message(arr, side).start())
 
     def halo_stats(arr):
         for side, start in ((0, dst_off), (1, dst_on)):
-            message(arr, side).wait_recv()
+            each_side(side, lambda side=side: message(arr, side).wait_recv())
             rows = pl.ds(start, WINDOW)
             got = msg_in[arr, side]
             rstd[arr, rows] = jnp.broadcast_to(got[0:1], (WINDOW, HEAD)).T
@@ -233,8 +266,12 @@
         @pl.loop(0, GROUPS)
         def _(g):
             halo_on(arr, g).wait_recv()
-            halo_off(arr, g, 0, seg).wait_recv()
-            halo_off(arr, g, 1, seg).wait_recv()
+
+            @pl.when(inner)
+            def _():
+                halo_off(arr, g, 0, seg).wait_recv()
+                halo_off(arr, g, 1, seg).wait_recv()
+
             heads = [g * PACK + u for u in range(PACK)]
             for u, h in enumerate(heads):
                 shift = mods[h][mod_row : mod_row + 1]
@@ -243,23 +280,33 @@
                 normed = (raw * rstd[arr] + offset[arr]) * scale + shift
                 keys[u, :, :HEAD] = normed.astype(BF16)
             results = []
-            for u, h in enumerate(heads):
-                gate = mods[2 * HEADS + h][mod_row : mod_row + 1]
-                attn = attend(u)
-                for b in range(2):
-                    own = x[arr][h, rows_of(b)].astype(F32)
-                    part = attn[b * WINDOW : (b + 1) * WINDOW]
-                    results.append((h, b, own + gate * part))
+            scores, expo = {}, {}
+            for step in range(PACK + 2):
+                if step < PACK:
+                    scores[step] = products(step)
+                if 1 <= step <= PACK:
+                    expo[step - 1] = weights(scores.pop(step - 1))
+                if step >= 2:
+                    u = step - 2
+                    h = heads[u]
+                    gate = mods[2 * HEADS + h][mod_row : mod_row + 1]
+                    attn = mixed(u, expo.pop(u))
+                    for b in range(2):
+                        own = x[arr][h, rows_of(b)].astype(F32)
+                        part = attn[b * WINDOW : (b + 1) * WINDOW]
+                        results.append((h, b, own + gate * part))
             finish(results)
             after(g)
 
-    def attend(u):
-        scores = lax.dot_general(
+    def products(u):
+        return lax.dot_general(
             keys[u, WINDOW : WINDOW + ROWS, :HEAD],
             keys[u, :, :HEAD],
             (((1,), (1,)), ((), ())),
             preferred_element_type=F32,
         )
+
+    def weights(scores):
         blocks = []
         none = jnp.zeros((WINDOW, WINDOW), BF16)
         for b in range(2):
@@ -270,7 +317,10 @@
             top = jnp.max(jnp.maximum(jnp.maximum(left, right), mid), axis=1, keepdims=True)
             expo = [jnp.exp2(part - top).astype(BF16) for part in (left, mid, right)]
             blocks.append(jnp.concatenate([none] * b + expo + [none] * (1 - b), axis=1))
-        both = jnp.dot(jnp.concatenate(blocks, axis=0), keys[u], preferred_element_type=F32)
+        return jnp.concatenate(blocks, axis=0)
+
+    def mixed(u, expo):
+        both = jnp.dot(expo, keys[u], preferred_element_type=F32)
         return both[:, :HEAD] * pl.reciprocal(both[:, HEAD:], approx=True)
 
     def rows_of(b):
@@ -278,13 +328,10 @@
 
     for k in range(1, 8):
         mod1(k).start()
+    tell(True, True)
     wait_load(LATENT)
-    send_all(LATENT)
-    for k in range(1, 8):
-        mod1(k).wait_recv()
-    for k in range(1, 4):
-        mod2(k).start()
-
+    send_groups(LATENT, 0, 2)
+    load(STALE, stale_hbm)
     keys[:, :, HEAD:] = jnp.ones((PACK, EXT, HEAD), BF16)
     query_at = lax.broadcasted_iota(jnp.int32, (WINDOW, WINDOW), 0)
     key_at = lax.broadcasted_iota(jnp.int32, (WINDOW, WINDOW), 1)
@@ -294,14 +341,39 @@
     bias[1] = right_bias
     bias[2] = left_bias
     bias[3] = jnp.where(seq == last, MASKED, right_bias)
+
+    @pl.when(jnp.logical_not(inner))
+    def _():
+        none = pl.ds(dst_on, WINDOW)
+        for arr in range(4):
+            msg_in[arr, 1] = jnp.zeros((8, HEAD), F32)
+
+            @pl.loop(0, HEADS)
+            def _(h, arr=arr):
+                x[arr][h, none] = jnp.zeros((WINDOW, HEAD), BF16)
+
     own_stats(LATENT)
+    pl.semaphore_wait(from_below, 1)
+    pl.semaphore_wait(from_above, 1)
+    tell(True, True)
+    for k in range(1, 8):
+        mod1(k).wait_recv()
+    joint[across] = (plane[:4] + plane[4:])[:, :4]
+    for k in range(1, 4):
+        mod2(k).start()
+    send_groups(LATENT, 2, 4)
+    wait_load(STALE)
+    pl.semaphore_wait(from_below, 1)
+    pl.semaphore_wait(from_above, 1)
+    tell(True, False)
+    own_stats(STALE)
 
     for k in range(1, 4):
         mod2(k).wait_recv()
     lane = lax.broadcasted_iota(jnp.int32, (8, HEAD), 1)
 
     def chunk(k):
-        return plane[k // 4, k % 4] + plane[k // 4, 4 + k % 4]
+        return jnp.concatenate([joint[k // 4, k % 4], jnp.zeros((4, HEAD), F32)], axis=0)
 
     for k in range(PLANE):
         first, second = chunk(k), chunk(k + 1)
@@ -313,12 +385,12 @@
         factor = jnp.where(at < 2 * HEADS, F32(ROOT), F32(1.0 / ROOT))
         row = (row + jnp.where(at // HEADS == 1, F32(1.0), F32(0.0))) * factor
         mods[at] = row[:4]
+    pl.semaphore_wait(from_below, 1)
     for k in range(1, 8):
         mod3(k).start()
 
-    wait_load(STALE)
-    send_all(STALE)
-    own_stats(STALE)
+    send_groups(LATENT, 4, GROUPS)
+    send_groups(STALE, 0, GROUPS)
     for k in range(1, 8):
         mod3(k).wait_recv()
 
@@ -349,12 +421,19 @@
 
         return after
 
+    def early(g):
+        @pl.when(g < EARLY)
+        def _():
+            send_halo(FRESH, g)
+
     halo_stats(LATENT)
-    run_section(LATENT, 0, to_fresh, functools.partial(send_halo, FRESH))
+    run_section(LATENT, 0, to_fresh, early)
     own_stats(FRESH)
+    send_groups(FRESH, EARLY, GROUPS)
     halo_stats(STALE)
-    run_section(STALE, 2, to_state, functools.partial(send_halo, STATE))
+    run_section(STALE, 2, to_state, lambda g: None)
     own_stats(STATE)
+    send_groups(STATE, 0, GROUPS)
     halo_stats(FRESH)
     run_section(FRESH, 3, to_latent_out, write(0, latent_out))
     halo_stats(STATE)
@@ -369,10 +448,13 @@
         mod2(k).wait_send()
     for arr in range(4):
         for side in range(2):
-            message(arr, side).wait_send()
+            each_side(side, lambda side=side, arr=arr: message(arr, side).wait_send())
         sent = x[arr].at[:, pl.ds(0, WINDOW)]
         pltpu.make_async_copy(sent, sent, send_on.at[arr]).wait()
-        pltpu.make_async_copy(sent, sent, send_off.at[arr]).wait()
+
+        @pl.when(inner)
+        def _(arr=arr, sent=sent):
+            pltpu.make_async_copy(sent, sent, send_off.at[arr]).wait()
 
 
 def per_device(latent, stale_hidden, step_ids, sigma_table, mod_weight):
@@ -394,7 +476,8 @@
             pltpu.VMEM((PACK, EXT, 2 * HEAD), BF16),
             pltpu.VMEM((4, 2, 8, HEAD), F32),
             pltpu.VMEM((4, 2, 8, HEAD), F32),
-            pltpu.VMEM((4, 8, 8, HEAD), F32),
+            pltpu.VMEM((8, 8, HEAD), F32),
+            pltpu.VMEM((4, 4, 4, HEAD), F32),
             pltpu.VMEM((3 * HEADS, 4, HEAD), F32),
             dma((2,)),
             dma((2,)),
@@ -410,11 +493,13 @@
             dma((4,)),
             dma((8,)),
             dma((8,)),
+            pltpu.SemaphoreType.REGULAR,
+            pltpu.SemaphoreType.REGULAR,
         ],
         compiler_params=pltpu.CompilerParams(
             collective_id=0, has_side_effects=True, vmem_limit_bytes=48 * 1024 * 1024
         ),
-    )(latent, stale_hidden, step_ids, sigma_table, mod_weight)
+    )(latent, stale_hidden, step_ids, sigma_table, jnp.swapaxes(mod_weight, 1, 2))
 
 
 def solution(mesh):

time: 91.5 us -> 81.2 us (0.89)
  Pallas kernels: 84.9 us -> 75.2 us
    pallas_call x1, Pallas kernels: 84.9 us -> 75.2 us  [per_device(): pl.pallas_call(kernel, out_shape=(result, result), in_specs=[anywhere, an...]
    unnamed x7 -> x8, local copies, waits for them, and re-layouts: 5.27 us -> 5.15 us
where the time goes in v3:
time: 81.2 us; the launch traced here: 81 us
  Pallas kernels  75.2 us (93%)
  local copies, waits for them, and re-layouts  5.15 us (6%)
    pallas_call x1, Pallas kernels, per_device(): pl.pallas_call(kernel, out_shape=(result, result), in_specs=[anywhere, an...  75.2 us
    unnamed x8, local copies, waits for them, and re-layouts  5.15 us

profile of v3, /device:TPU:32, one launch (start us, length us, event | category | flops | bytes accessed | tf_op | source)
XLA Modules:
  0.0 81.0 jit_solution(9831984978471806984)
XLA Ops:
  0.6 0.0 copy-start
  0.6 0.8 %copy-done = bf16[1,256,120]{1,2,0:T(8,128)(2,1)S(1)} copy-done((bf16[1,256,120]{1,2,0:T(8,128)(2,1)S(1)}, bf16[1,256,120]{1,2,0:T(8,128)(2,1)}, u32[]{:S(2)}) %copy-start) | copy-done | bytes 61464
  1.5 0.0 copy-start.1
  1.5 0.7 copy-done.1
  2.1 0.0 copy-start.2
  2.2 0.7 copy-done.2
  2.8 75.2 %shard_map.68 = (bf16[256,5120]{1,0:T(8,128)(2,1)S(1)}, bf16[256,5120]{1,0:T(8,128)(2,1)S(1)}) custom-call(bf16[256,5120]{1,0:T(8,128)(2,1)} %latent_hbm.1, bf16[256,5120]{1,0:T(8,128)(2,1)} %stale_hbm.1, s32[3]{0:T(128)S(1)} %copy-done.2, s32[1000]{0:T(1024)S(1)} %copy-done.1, bf16[1,120,256]{2,1,0:T(8,128)(2,1)S(1)} %bitcast.1), custom_call_target="tpu_custom_call" | custom-call | tf_op jit(solution)/shard_map/pallas_call | solution.py:465
  78.0 1.5 %copy.9 = bf16[256,5120]{1,0:T(8,128)(2,1)} copy(bf16[256,5120]{1,0:T(8,128)(2,1)S(1)} %get-tuple-element.4) | data formatting | bytes 5242880
  79.5 1.5 %copy.10 = bf16[256,5120]{1,0:T(8,128)(2,1)} copy(bf16[256,5120]{1,0:T(8,128)(2,1)S(1)} %get-tuple-element.5) | data formatting | bytes 5242880
Async XLA Ops:
  0.6 0.8 %copy-start = (bf16[1,256,120]{1,2,0:T(8,128)(2,1)S(1)}, bf16[1,256,120]{1,2,0:T(8,128)(2,1)}, u32[]{:S(2)}) copy-start(bf16[1,256,120]{1,2,0:T(8,128)(2,1)} %param.9) | copy-start | bytes 184324
  1.5 0.7 copy-start.1
  2.1 0.7 copy-start.2

commit v4 on v3

--- a/solution.py
+++ b/solution.py
@@ -43,9 +43,9 @@
 def kernel(
     latent_hbm,
     stale_hbm,
-    step_ids,
-    sigma_table,
-    weight,
+    step_ids_hbm,
+    sigma_hbm,
+    weight_hbm,
     latent_out,
     hidden_out,
     x_latent,
@@ -79,6 +79,10 @@
     send_mod3,
     from_below,
     from_above,
+    step_ids,
+    sigma_table,
+    weight,
+    small_sem,
 ):
     x = (x_latent, x_stale, x_fresh, x_state)
     out = (out_latent, out_hidden)
@@ -120,6 +124,15 @@
         whole = x[arr].at[:, pl.ds(WINDOW, ROWS)]
         pltpu.make_async_copy(whole, whole, load_sem.at[arr]).wait()
 
+    small = [
+        pltpu.make_async_copy(source, target, small_sem.at[i])
+        for i, (source, target) in enumerate(
+            ((step_ids_hbm, step_ids), (sigma_hbm, sigma_table), (weight_hbm, weight))
+        )
+    ]
+    for copy in small:
+        copy.start()
+
     inner = (seq > 0) & (seq < last)
     above, below = peer_deep(1), peer_deep(7)
     barrier = pltpu.get_barrier_semaphore()
@@ -136,6 +149,8 @@
         pl.semaphore_signal(barrier, inc=1, device_id=partner, device_id_type=MESH)
     load(LATENT, latent_hbm)
 
+    for copy in small:
+        copy.wait()
     times = [sigma_table[step_ids[i]].astype(F32) for i in range(3)]
     feats = features(times[0], times[1], seg)
     columns = lax.dot_general(
@@ -457,15 +472,27 @@
             pltpu.make_async_copy(sent, sent, send_off.at[arr]).wait()
 
 
+def write_out(first, second, first_out, second_out, sem):
+    copies = [
+        pltpu.make_async_copy(first, first_out, sem.at[0]),
+        pltpu.make_async_copy(second, second_out, sem.at[1]),
+    ]
+    for copy in copies:
+        copy.start()
+    for copy in copies:
+        copy.wait()
+
+
 def per_device(latent, stale_hidden, step_ids, sigma_table, mod_weight):
     dma = pltpu.SemaphoreType.DMA
     anywhere = pl.BlockSpec(memory_space=pl.ANY)
-    scalars = pl.BlockSpec(memory_space=pltpu.SMEM)
+    fixed = pl.BlockSpec(memory_space=pltpu.HBM)
+    weight = jnp.swapaxes(mod_weight, 1, 2)
     result = jax.ShapeDtypeStruct(latent.shape, latent.dtype)
-    return pl.pallas_call(
+    results = pl.pallas_call(
         kernel,
         out_shape=(result, result),
-        in_specs=[anywhere, anywhere, scalars, scalars, pl.BlockSpec(memory_space=pltpu.VMEM)],
+        in_specs=[anywhere, anywhere, fixed, fixed, fixed],
         out_specs=(anywhere, anywhere),
         scratch_shapes=[
             *[pltpu.VMEM((HEADS, EXT, HEAD), BF16)] * 4,
@@ -495,11 +522,23 @@
             dma((8,)),
             pltpu.SemaphoreType.REGULAR,
             pltpu.SemaphoreType.REGULAR,
+            pltpu.SMEM(step_ids.shape, jnp.int32),
+            pltpu.SMEM(sigma_table.shape, jnp.int32),
+            pltpu.VMEM(weight.shape, BF16),
+            dma((3,)),
         ],
         compiler_params=pltpu.CompilerParams(
             collective_id=0, has_side_effects=True, vmem_limit_bytes=48 * 1024 * 1024
         ),
-    )(latent, stale_hidden, step_ids, sigma_table, jnp.swapaxes(mod_weight, 1, 2))
+    )(latent, stale_hidden, *[pltpu.with_memory_space_constraint(v, pltpu.HBM) for v in (step_ids, sigma_table, weight)])
+    return pl.pallas_call(
+        write_out,
+        out_shape=(result, result),
+        in_specs=[anywhere, anywhere],
+        out_specs=(fixed, fixed),
+        scratch_shapes=[dma((2,))],
+        compiler_params=pltpu.CompilerParams(vmem_limit_bytes=1024 * 1024),
+    )(*results)
 
 
 def solution(mesh):

time: 81.2 us -> 78 us (0.961)
  local copies, waits for them, and re-layouts: 5.15 us -> 0 us
  Pallas kernels: 75.2 us -> 77.1 us
    unnamed x8 -> x0, local copies, waits for them, and re-layouts: 5.15 us -> none
    pallas_call x0 -> x1, Pallas kernels: none -> 2.37 us  [per_device(): pl.pallas_call(write_out, out_shape=(result, result), in_specs=[anywhere,...]
where the time goes in v4:
time: 78 us; the launch traced here: 77.8 us
  Pallas kernels  77.1 us (99%)
    pallas_call x1, Pallas kernels, per_device(): pl.pallas_call(kernel, out_shape=(result, result), in_specs=[anywhere, an...  74.8 us
    pallas_call x1, Pallas kernels, per_device(): pl.pallas_call(write_out, out_shape=(result, result), in_specs=[anywhere,...  2.37 us

profile of v4, /device:TPU:32, one launch (start us, length us, event | category | flops | bytes accessed | tf_op | source)
XLA Modules:
  0.0 77.8 jit_solution(7342448481047878038)
XLA Ops:
  0.6 74.8 %shard_map.68 = (bf16[256,5120]{1,0:T(8,128)(2,1)S(1)}, bf16[256,5120]{1,0:T(8,128)(2,1)S(1)}) custom-call(bf16[256,5120]{1,0:T(8,128)(2,1)} %latent_hbm.1, bf16[256,5120]{1,0:T(8,128)(2,1)} %stale_hbm.1, s32[3]{0:T(128)} %step_ids_hbm.1, s32[1000]{0:T(1024)} %sigma_hbm.1, bf16[1,120,256]{2,1,0:T(8,128)(2,1)} %bitcast.1), custom_call_target="tpu_custom_call" | custom-call | tf_op jit(solution)/shard_map/pallas_call | solution.py:492
  75.4 2.4 %shard_map.69 = (bf16[256,5120]{1,0:T(8,128)(2,1)}, bf16[256,5120]{1,0:T(8,128)(2,1)}) custom-call(bf16[256,5120]{1,0:T(8,128)(2,1)S(1)} %get-tuple-element.4.first, bf16[256,5120]{1,0:T(8,128)(2,1)S(1)} %get-tuple-element.5.second), custom_call_target="tpu_custom_call" | custom-call | tf_op jit(solution)/shard_map/pallas_call | solution.py:534

commit v5 on v4

--- a/solution.py
+++ b/solution.py
@@ -13,7 +13,7 @@
 ROWS = 256
 EXT = ROWS + 2 * WINDOW
 WIDTH = HEADS * HEAD
-PACK = 8
+PACK = 10
 GROUPS = HEADS // PACK
 COLS = 120
 PLANE = 15
@@ -214,12 +214,12 @@
         )
 
     def send_halo(arr, g):
-        halo_on(arr, g).start()
-
         @pl.when(inner)
         def _():
             halo_off(arr, g, seg, 0).start()
             halo_off(arr, g, seg, 1).start()
+
+        halo_on(arr, g).start()
 
     def send_groups(arr, first, end):
         @pl.loop(first, end)
@@ -376,12 +376,11 @@
     joint[across] = (plane[:4] + plane[4:])[:, :4]
     for k in range(1, 4):
         mod2(k).start()
-    send_groups(LATENT, 2, 4)
+    send_groups(LATENT, 2, 3)
     wait_load(STALE)
     pl.semaphore_wait(from_below, 1)
     pl.semaphore_wait(from_above, 1)
     tell(True, False)
-    own_stats(STALE)
 
     for k in range(1, 4):
         mod2(k).wait_recv()
@@ -404,8 +403,9 @@
     for k in range(1, 8):
         mod3(k).start()
 
-    send_groups(LATENT, 4, GROUPS)
+    send_groups(LATENT, 3, GROUPS)
     send_groups(STALE, 0, GROUPS)
+    own_stats(STALE)
     for k in range(1, 8):
         mod3(k).wait_recv()
 

time: 78 us -> 77.9 us (level)
  no operation moved by 1% of the time
where the time goes in v5:
time: 77.9 us; the launch traced here: 77.7 us
  Pallas kernels  77 us (99%)
    pallas_call x1, Pallas kernels, per_device(): pl.pallas_call(kernel, out_shape=(result, result), in_specs=[anywhere, an...  74.7 us
    pallas_call x1, Pallas kernels, per_device(): pl.pallas_call(write_out, out_shape=(result, result), in_specs=[anywhere,...  2.37 us

profile of v5, /device:TPU:32, one launch (start us, length us, event | category | flops | bytes accessed | tf_op | source)
XLA Modules:
  0.0 77.7 jit_solution(16415385393326893928)
XLA Ops:
  0.6 74.7 %shard_map.68 = (bf16[256,5120]{1,0:T(8,128)(2,1)S(1)}, bf16[256,5120]{1,0:T(8,128)(2,1)S(1)}) custom-call(bf16[256,5120]{1,0:T(8,128)(2,1)} %latent_hbm.1, bf16[256,5120]{1,0:T(8,128)(2,1)} %stale_hbm.1, s32[3]{0:T(128)} %step_ids_hbm.1, s32[1000]{0:T(1024)} %sigma_hbm.1, bf16[1,120,256]{2,1,0:T(8,128)(2,1)} %bitcast.1), custom_call_target="tpu_custom_call" | custom-call | tf_op jit(solution)/shard_map/pallas_call | solution.py:492
  75.3 2.4 %shard_map.69 = (bf16[256,5120]{1,0:T(8,128)(2,1)}, bf16[256,5120]{1,0:T(8,128)(2,1)}) custom-call(bf16[256,5120]{1,0:T(8,128)(2,1)S(1)} %get-tuple-element.4.first, bf16[256,5120]{1,0:T(8,128)(2,1)S(1)} %get-tuple-element.5.second), custom_call_target="tpu_custom_call" | custom-call | tf_op jit(solution)/shard_map/pallas_call | solution.py:534
